TPU v7x, 512 devices: a whole 4x8x8 slice. The times are simulated.
512 devices in a mesh: sec: 8 (over y), rad: 16 (over z, x_hi), ax: 4 (over x_lo, core).
Axes of the slice: x: 4 (x_hi: 2, x_lo: 2; x = x_hi * 2 + x_lo), y: 8, z: 8, core: 2. Of those that a mesh axis runs over, the one named last changes fastest.
Arguments:
- state: float32 [5, 8, 1024, 2048], P(None, 'ax', 'rad', 'sec'), may hold values from -1.6 to 4, as said below
- coarsen: int32 [16], replicated, may hold values from 1 to 16, as said below
Outputs:
- tendency: float32 [5, 8, 1024, 2048], P(None, 'ax', 'rad', 'sec')
Inputs may be any that keep to these rules, and one draw needn't show every extreme that they name: `coarsen`: each entry is a power of two; cycle 0 takes 16 and cycle 16 - 1 takes 1. state[0] (density) lies in 0.6 to 1.4, the momenta in -1.6 to 1.6, state[4] (energy) in 2.5 to 4.0.
All inputs are finite; a program needn't handle non-finite values.
Results may differ from a plain program's by a relative error of at most 0.0003.
Values sent between devices are 32-bit elements; how exact they have to be, the bound alone decides.
A program may use at most 64 MiB of HBM per device.

v0:
```python
import math
import jax
import jax.numpy as jnp
from jax import lax
from jax.sharding import PartitionSpec as P

R_NEAR = 16
GAMMA = 1.4
KAPPA = 1.44


def padded_2(value, sides, width):
    for axis, dim in sides:
        size, length = (lax.axis_size(axis), value.shape[dim])
        up = [(i, (i + 1) % size) for i in range(size)]
        down = [(j, i) for i, j in up]
        last = lax.slice_in_dim(value, length - width, length, axis=dim)
        first = lax.slice_in_dim(value, 0, width, axis=dim)
        before = lax.ppermute(last, axis, up)
        after = lax.ppermute(first, axis, down)
        value = jnp.concatenate([before, value, after], axis=dim)
    return value


def spread(value, axis, root):
    mine = lax.axis_index(axis) == root
    return lax.psum(jnp.where(mine, value, jnp.zeros_like(value)), axis)


def body(state, coarsen):
    fields, planes, cycles_dev, cells_dev = state.shape
    sec_count = lax.axis_size("sec")
    rad_count = lax.axis_size("rad")
    ax_count = lax.axis_size("ax")
    sec_index = lax.axis_index("sec")
    rad_index = lax.axis_index("rad")
    ax_index = lax.axis_index("ax")
    total_cells = cells_dev * sec_count
    dtheta = 2.0 * math.pi / total_cells
    padded = padded_2(state, (("sec", 3), ("rad", 2), ("ax", 1)), 1)
    plane_pos = ax_index * planes + jnp.arange(-1, planes + 1, dtype=jnp.int32)
    cycle_pos = rad_index * cycles_dev + jnp.arange(-1, cycles_dev + 1, dtype=jnp.int32)
    inside_ax = ((plane_pos >= 0) & (plane_pos < planes * ax_count)).astype(jnp.float32)
    inside_rad = ((cycle_pos >= 0) & (cycle_pos < cycles_dev * rad_count)).astype(jnp.float32)
    ghost_plane = jnp.arange(planes + 2) % (planes + 1) == 0
    ghost_cycle = jnp.arange(cycles_dev + 2) % (cycles_dev + 1) == 0
    ghost_cell = jnp.arange(cells_dev + 2) % (cells_dev + 1) == 0
    ghosts = (
        ghost_plane.astype(jnp.int32)[:, None, None]
        + ghost_cycle.astype(jnp.int32)[None, :, None]
        + ghost_cell.astype(jnp.int32)[None, None, :]
    )
    corner = ghosts >= 2
    density = jnp.where(corner, 1.0, padded[0])
    mom_ax = padded[1]
    mom_rad = padded[2]
    mom_az = padded[3]
    energy = padded[4]
    vel_ax = mom_ax / density
    vel_rad = mom_rad / density
    vel_az = mom_az / density
    pressure = (GAMMA - 1.0) * (
        energy - 0.5 * (mom_ax * vel_ax + mom_rad * vel_rad + mom_az * vel_az)
    )
    radius_pad = cycle_pos.astype(jnp.float32) + 0.5
    flux_ax = jnp.stack(
        [
            mom_ax,
            mom_ax * vel_ax + pressure,
            mom_rad * vel_ax,
            mom_az * vel_ax,
            (energy + pressure) * vel_ax,
        ]
    )
    flux_ax = flux_ax * inside_ax[None, :, None, None]
    flux_rad = jnp.stack(
        [
            mom_rad,
            mom_ax * vel_rad,
            mom_rad * vel_rad + pressure,
            mom_az * vel_rad,
            (energy + pressure) * vel_rad,
        ]
    )
    flux_rad = flux_rad * (radius_pad * inside_rad)[None, None, :, None]
    flux_az = jnp.stack(
        [
            mom_az,
            mom_ax * vel_az,
            mom_rad * vel_az,
            mom_az * vel_az + pressure,
            (energy + pressure) * vel_az,
        ]
    )
    radius = radius_pad[1:-1][:, None]
    tendency = -(flux_ax[:, 2:, 1:-1, 1:-1] - flux_ax[:, :-2, 1:-1, 1:-1]) * 0.5
    tendency = (
        tendency - (flux_rad[:, 1:-1, 2:, 1:-1] - flux_rad[:, 1:-1, :-2, 1:-1]) * 0.5 / radius
    )
    tendency = tendency - (flux_az[:, 1:-1, 1:-1, 2:] - flux_az[:, 1:-1, 1:-1, :-2]) * 0.5 / (
        radius * dtheta
    )
    inner_press = pressure[1:-1, 1:-1, 1:-1]
    inner_mom_az = mom_az[1:-1, 1:-1, 1:-1]
    inner_mom_rad = mom_rad[1:-1, 1:-1, 1:-1]
    inner_vel_az = vel_az[1:-1, 1:-1, 1:-1]
    zero_part = jnp.zeros_like(inner_press)
    source = jnp.stack(
        [
            zero_part,
            zero_part,
            (inner_press + inner_mom_az * inner_vel_az) / radius,
            -(inner_mom_rad * inner_vel_az) / radius,
            zero_part,
        ]
    )
    tendency = tendency + source
    own_pos = sec_index * cells_dev + jnp.arange(cells_dev, dtype=jnp.int32)

    def kernel(cycle_factor, cycle_blocks, log_ratio, scale_const, columns):
        rows_coarse = own_pos // cycle_factor
        columns_coarse = columns // cycle_factor
        distance = ((rows_coarse[:, None] - columns_coarse[None, :]) % cycle_blocks).astype(
            jnp.float32
        )
        blocks_f = cycle_blocks.astype(jnp.float32)
        return (jnp.exp(distance * log_ratio) + jnp.exp((blocks_f - distance) * log_ratio)) / (
            scale_const * cycle_factor.astype(jnp.float32)
        )

    near_axis = tendency[:, :, :R_NEAR, :]
    cycle_lines = jnp.transpose(near_axis, (2, 0, 1, 3)).reshape(R_NEAR, fields * planes, cells_dev)
    shared = spread(cycle_lines, "rad", 0)
    per_device = R_NEAR // rad_count
    my_cycles = lax.dynamic_slice_in_dim(shared, rad_index * per_device, per_device, 0)
    selector = (rad_index * per_device + jnp.arange(per_device, dtype=jnp.int32))[
        :, None
    ] == jnp.arange(coarsen.shape[0], dtype=jnp.int32)[None, :]
    factor = jnp.sum(jnp.where(selector, coarsen[None, :], 0), axis=1)
    blocks = total_cells // factor
    factor_f = factor.astype(jnp.float32)
    stiffness = KAPPA / (factor_f * dtheta) ** 2
    inverse_half = 0.5 / stiffness
    one_minus = jnp.sqrt(inverse_half * (2.0 + inverse_half)) - inverse_half
    log_ratio = jnp.log1p(-one_minus)
    scale_const = (
        stiffness
        * one_minus
        * (2.0 - one_minus)
        / (1.0 - one_minus)
        * -jnp.expm1(blocks.astype(jnp.float32) * log_ratio)
    )
    portion = lax.all_gather(my_cycles, "sec", axis=2, tiled=True)
    columns = jnp.arange(portion.shape[2], dtype=jnp.int32)

    def per_cycle(cycle_item):
        lines_one, cycle_factor, cycle_blocks, cycle_log, cycle_scale = cycle_item
        table = kernel(cycle_factor, cycle_blocks, cycle_log, cycle_scale, columns)
        return jnp.einsum("lq,pq->lp", lines_one, table, precision=lax.Precision.HIGHEST)

    smoothed = lax.map(per_cycle, (portion, factor, blocks, log_ratio, scale_const))
    result = lax.all_gather(smoothed, "rad", axis=0, tiled=True)
    restored = jnp.transpose(result.reshape(R_NEAR, fields, planes, cells_dev), (1, 2, 0, 3))
    near_new = jnp.where(rad_index == 0, restored, near_axis)
    return jnp.concatenate([near_new, tendency[:, :, R_NEAR:, :]], axis=2)


def solution(mesh):
    return jax.shard_map(
        body,
        mesh=mesh,
        in_specs=(P(None, "ax", "rad", "sec"), P()),
        out_specs=P(None, "ax", "rad", "sec"),
        check_vma=False,
    )
```

profile of v0, /device:TPU:6, one launch (start us, length us, event | category | flops | bytes accessed | tf_op | source)
XLA Modules:
  0.0 309.1 jit_solution(6789559779002969412)
XLA Ops:
  6.5 1.3 fusion.47
  7.8 3.5 %collective-permute-start = (f32[5,2,64,1]{3,2,1,0:T(8,128)S(1)}, f32[5,2,64,1]{3,2,1,0:T(8,128)S(1)}, u32[]{:S(2)}, u32[]{:S(2)}) collective-permute-start(f32[5,2,64,1]{3,2,1,0:T(8,128)S(1)} %get-tuple-element.59), channel_id=1, source_target_pairs={{0,64},{64,128},{128,192},{192,256},{256,320},{320,384},{384,448},... | collective-permute-start | bytes 7688 | tf_op jit(solution)/shard_map/ppermute | solution.py:19
  11.3 3.8 %collective-permute-start.1 = (f32[5,2,64,1]{3,2,1,0:T(8,128)S(1)}, f32[5,2,64,1]{3,2,1,0:T(8,128)S(1)}, u32[]{:S(2)}, u32[]{:S(2)}) collective-permute-start(f32[5,2,64,1]{3,2,1,0:T(8,128)S(1)} %get-tuple-element.60), channel_id=1, source_target_pairs={{64,0},{128,64},{192,128},{256,192},{320,256},{384,320},{448,384},... | collective-permute-start | bytes 7688 | tf_op jit(solution)/shard_map/ppermute | solution.py:20
  15.2 1.4 fusion.44
  16.6 4.3 %collective-permute-done = f32[5,2,64,1]{3,2,1,0:T(8,128)S(1)} collective-permute-done((f32[5,2,64,1]{3,2,1,0:T(8,128)S(1)}, f32[5,2,64,1]{3,2,1,0:T(8,128)S(1)}, u32[]{:S(2)}, u32[]{:S(2)}) %collective-permute-start) | collective-permute-done | bytes 2592 | tf_op jit(solution)/shard_map/ppermute | solution.py:19
  20.9 1.5 collective-permute-done.1
  22.4 1.1 pad_maximum_fusion.5
  23.5 5.1 %collective-permute-start.2 = (f32[5,2,1,258]{3,2,1,0:T(1,128)S(1)}, f32[5,2,1,258]{3,2,1,0:T(1,128)S(1)}, u32[]{:S(2)}, u32[]{:S(2)}) collective-permute-start(f32[5,2,1,258]{3,2,1,0:T(1,128)S(1)} %get-tuple-element.53), channel_id=1, source_target_pairs={{0,4},{4,8},{8,12},{12,16},{16,20},{20,24},{24,28},{28,32},{32,36}... | collective-permute-start | bytes 30968 | tf_op jit(solution)/shard_map/ppermute | solution.py:19
  28.6 2.2 collective-permute-start.3
  30.9 5.8 %collective-permute-done.3 = f32[5,2,1,258]{3,2,1,0:T(1,128)S(1)} collective-permute-done((f32[5,2,1,258]{3,2,1,0:T(1,128)S(1)}, f32[5,2,1,258]{3,2,1,0:T(1,128)S(1)}, u32[]{:S(2)}, u32[]{:S(2)}) %collective-permute-start.3) | collective-permute-done | bytes 10352 | tf_op jit(solution)/shard_map/ppermute | solution.py:20
  36.6 0.5 pad_maximum_fusion.1
  37.2 0.5 copy.5
  37.7 1.9 collective-permute-start.4
  39.6 0.5 copy.6
  40.2 3.6 %collective-permute-start.5 = (f32[5,1,66,258]{3,1,2,0:T(1,128)S(1)}, f32[5,1,66,258]{3,1,2,0:T(1,128)S(1)}, u32[]{:S(2)}, u32[]{:S(2)}) collective-permute-start(f32[5,1,66,258]{3,1,2,0:T(1,128)S(1)} %copy.6), channel_id=1, source_target_pairs={{1,0},{2,1},{3,2},{0,3},{5,4},{6,5},{7,6},{4,7},{9,8},{10,9},{11,1... | collective-permute-start | bytes 1021688 | tf_op jit(solution)/shard_map/ppermute | solution.py:20
  44.7 6.0 %collective-permute-done.4 = f32[5,1,66,258]{3,1,2,0:T(1,128)S(1)} collective-permute-done((f32[5,1,66,258]{3,1,2,0:T(1,128)S(1)}, f32[5,1,66,258]{3,1,2,0:T(1,128)S(1)}, u32[]{:S(2)}, u32[]{:S(2)}) %collective-permute-start.4) | collective-permute-done | bytes 340592 | tf_op jit(solution)/shard_map/ppermute | solution.py:19
  51.0 0.5 pad_maximum_fusion
  51.5 0.2 slice_bitcast_fusion.3
  51.9 0.3 add_dynamic-update-slice_fusion.2
  52.5 0.2 multiply_dynamic-update-slice_fusion.6
  52.9 0.4 broadcast_multiply_fusion
  53.3 0.3 fusion.32
  53.6 1.1 fusion.19
  54.7 0.7 slice_select_fusion.1
  55.4 0.8 and_select_fusion
  58.5 0.8 add_select_fusion.1
  59.4 161.4 %all-reduce.2.cloned.1.call-done = f32[16,10,256]{2,0,1:T(8,128)} async-done(((f32[16,10,256]{2,0,1:T(8,128)}), f32[16,10,256]{2,0,1:T(8,128)}) %all-reduce.2.cloned.1.call-update) | async-done | bytes 163856 | tf_op jit(solution)/shard_map/psum | solution.py:27
  220.8 0.9 constant_dynamic-slice_fusion
  221.7 16.7 %all_gather.6 = f32[1,10,2048]{2,0,1:T(1,128)S(1)} all-gather(f32[1,10,256]{2,0,1:T(1,128)S(1)} %constant_dynamic-slice_fusion), channel_id=1, replica_groups=mesh['sec'=8,'rad'=16,'ax'=4] {'sec'}, dimensions={2}, use_global_device_ids=true | all-gather | bytes 92160 | tf_op jit(solution)/shard_map/all_gather | solution.py:153
  238.4 22.6 %fusion.7 = f32[1,10,256]{2,1,0:T(8,128)S(1)} fusion(f32[]{:T(128)S(6)} %mul.233, f32[]{:T(128)S(6)} %convert_element_type.66, f32[]{:T(128)} %bitcast.13, s32[]{:T(128)S(6)} %select_n.132, s32[2048]{0:T(1024)S(1)} %add_select_fusion.1, s32[256]{0:T(256)S(1)} %and_select_fusion, pred[]{:T(512)S(6)} %lt.63, f32[1,10,2048]{2,0,1:T(1,128)S(1)} %all_gather.6), kind=kOutput, calls=%fused_computation.10 | convolution fusion | flops 70254592 | bytes 101393 | tf_op jit(solution)/shard_map/while/body/eval_jaxpr/lq,pq->lp/dot_general | solution.py:159
  261.0 40.3 %all-gather.1 = f32[16,10,256]{2,1,0:T(8,128)S(1)} all-gather(f32[1,10,256]{2,1,0:T(8,128)S(1)} %fusion.7), channel_id=2, replica_groups=mesh['sec'=8,'rad'=16,'ax'=4] {'rad'}, dimensions={0}, use_global_device_ids=true | all-gather | bytes 174080 | tf_op jit(solution)/shard_map/all_gather | solution.py:162
  301.4 0.9 pad_maximum_fusion.2
  (30 shorter events, 1.4 us)
Async XLA Ops:
  6.5 30.1 %copy-start = (f32[5,2,64,256]{3,2,1,0:T(8,128)S(1)}, f32[5,2,64,256]{3,2,1,0:T(8,128)}, u32[]{:S(2)}) copy-start(f32[5,2,64,256]{3,2,1,0:T(8,128)} %param.2) | copy-start | bytes 1966084
  6.5 214.2 %all-reduce.2.cloned.1.call-start = ((), (), s32[]{:S(2)}) async-start(), calls=%async_computation | async-start | bytes 327680 | tf_op jit(solution)/shard_map/psum | solution.py:27
  7.8 13.1 %collective-permute-start = (f32[5,2,64,1]{3,2,1,0:T(8,128)S(1)}, f32[5,2,64,1]{3,2,1,0:T(8,128)S(1)}, u32[]{:S(2)}, u32[]{:S(2)}) collective-permute-start(f32[5,2,64,1]{3,2,1,0:T(8,128)S(1)} %get-tuple-element.59), channel_id=1, source_target_pairs={{0,64},{64,128},{128,192},{192,256},{256,320},{320,384},{384,448},... | collective-permute-start | bytes 7688 | tf_op jit(solution)/shard_map/ppermute | solution.py:19
  11.3 11.1 %collective-permute-start.1 = (f32[5,2,64,1]{3,2,1,0:T(8,128)S(1)}, f32[5,2,64,1]{3,2,1,0:T(8,128)S(1)}, u32[]{:S(2)}, u32[]{:S(2)}) collective-permute-start(f32[5,2,64,1]{3,2,1,0:T(8,128)S(1)} %get-tuple-element.60), channel_id=1, source_target_pairs={{64,0},{128,64},{192,128},{256,192},{320,256},{384,320},{448,384},... | collective-permute-start | bytes 7688 | tf_op jit(solution)/shard_map/ppermute | solution.py:20
  23.5 7.4 %collective-permute-start.2 = (f32[5,2,1,258]{3,2,1,0:T(1,128)S(1)}, f32[5,2,1,258]{3,2,1,0:T(1,128)S(1)}, u32[]{:S(2)}, u32[]{:S(2)}) collective-permute-start(f32[5,2,1,258]{3,2,1,0:T(1,128)S(1)} %get-tuple-element.53), channel_id=1, source_target_pairs={{0,4},{4,8},{8,12},{12,16},{16,20},{20,24},{24,28},{28,32},{32,36}... | collective-permute-start | bytes 30968 | tf_op jit(solution)/shard_map/ppermute | solution.py:19
  28.6 8.0 %collective-permute-start.3 = (f32[5,2,1,258]{3,2,1,0:T(1,128)S(1)}, f32[5,2,1,258]{3,2,1,0:T(1,128)S(1)}, u32[]{:S(2)}, u32[]{:S(2)}) collective-permute-start(f32[5,2,1,258]{3,2,1,0:T(1,128)S(1)} %get-tuple-element.54), channel_id=1, source_target_pairs={{4,0},{8,4},{12,8},{16,12},{20,16},{24,20},{28,24},{32,28},{36,32}... | collective-permute-start | bytes 30968 | tf_op jit(solution)/shard_map/ppermute | solution.py:20
  37.7 13.0 %collective-permute-start.4 = (f32[5,1,66,258]{3,1,2,0:T(1,128)S(1)}, f32[5,1,66,258]{3,1,2,0:T(1,128)S(1)}, u32[]{:S(2)}, u32[]{:S(2)}) collective-permute-start(f32[5,1,66,258]{3,1,2,0:T(1,128)S(1)} %copy.5), channel_id=1, source_target_pairs={{0,1},{1,2},{2,3},{3,0},{4,5},{5,6},{6,7},{7,4},{8,9},{9,10},{10,1... | collective-permute-start | bytes 1021688 | tf_op jit(solution)/shard_map/ppermute | solution.py:19
  40.2 10.7 %collective-permute-start.5 = (f32[5,1,66,258]{3,1,2,0:T(1,128)S(1)}, f32[5,1,66,258]{3,1,2,0:T(1,128)S(1)}, u32[]{:S(2)}, u32[]{:S(2)}) collective-permute-start(f32[5,1,66,258]{3,1,2,0:T(1,128)S(1)} %copy.6), channel_id=1, source_target_pairs={{1,0},{2,1},{3,2},{0,3},{5,4},{6,5},{7,6},{4,7},{9,8},{10,9},{11,1... | collective-permute-start | bytes 1021688 | tf_op jit(solution)/shard_map/ppermute | solution.py:20
Sparse Core Ops, SparseCore 0:
  55.5 165.2 all-reduce.1
where the time goes:
time: 310 us; the launch traced here: 309 us
  waiting for transfers between devices  179 us (58%)
  blocking collectives  57 us (18%)
  matrix products  22.6 us (7%)
  starting transfers between devices  20.2 us (7%)
  between operations  16.7 us (5%)
  other arithmetic  9.79 us (3%)
  local copies, waits for them, and re-layouts  3.82 us (1%)
    psum x1, waiting for transfers between devices, spread(): return lax.psum(jnp.where(mine, value, jnp.zeros_like(value)), axis)  161 us
    all_gather x1, blocking collectives, body(): result = lax.all_gather(smoothed, 'rad', axis=0, tiled=True)  40.3 us
    dot_general x1, matrix products, per_cycle(): jnp.einsum('lq,pq->lp', lines_one, table, precision=lax.Precision.HIGHEST)  22.6 us
    all_gather x1, blocking collectives, body(): portion = lax.all_gather(my_cycles, 'sec', axis=2, tiled=True)  16.7 us
    ppermute x3, starting transfers between devices, padded_2(): before = lax.ppermute(last, axis, up)  10.5 us
    ppermute x3, waiting for transfers between devices, padded_2(): before = lax.ppermute(last, axis, up)  10.3 us
    ppermute x3, starting transfers between devices, padded_2(): after = lax.ppermute(first, axis, down)  9.68 us
    ppermute x3, waiting for transfers between devices, padded_2(): after = lax.ppermute(first, axis, down)  7.38 us
  transfers between devices with their start and end apart: 7, of which 6 were waited for; matrix products, arithmetic and copies ran while one was open for 1% of the time, Pallas kernels for 0%

commit v1 on v0

--- a/solution.py
+++ b/solution.py
@@ -7,6 +7,12 @@
 R_NEAR = 16
 GAMMA = 1.4
 KAPPA = 1.44
+
+
+def test_zone(obj, axis_id):
+    big = lax.all_gather(obj, axis_name=axis_id)
+    fresh = jnp.sum(big, axis=0)
+    return fresh
 
 
 def padded_2(value, sides, width):
@@ -24,7 +30,7 @@
 
 def spread(value, axis, root):
     mine = lax.axis_index(axis) == root
-    return lax.psum(jnp.where(mine, value, jnp.zeros_like(value)), axis)
+    return test_zone(jnp.where(mine, value, jnp.zeros_like(value)), axis)
 
 
 def body(state, coarsen):

time: 310 us -> 245 us (0.79)
  waiting for transfers between devices: 179 us -> 115 us
    psum x1 -> x0, waiting for transfers between devices: 161 us -> none  [spread(): return lax.psum(jnp.where(mine, value, jnp.zeros_like(value)), axis)]
    all_gather x0 -> x1, waiting for transfers between devices: none -> 95.5 us  [test_zone(): big = lax.all_gather(obj, axis_name=axis_id)]
where the time goes in v1:
time: 245 us; the launch traced here: 244 us
  waiting for transfers between devices  115 us (47%)
  blocking collectives  55.9 us (23%)
  matrix products  22.5 us (9%)
  starting transfers between devices  20.2 us (8%)
  between operations  16.1 us (7%)
  other arithmetic  10.8 us (4%)
  local copies, waits for them, and re-layouts  2.94 us (1%)
    all_gather x1, waiting for transfers between devices, test_zone(): big = lax.all_gather(obj, axis_name=axis_id)  95.5 us
    all_gather x1, blocking collectives, body(): result = lax.all_gather(smoothed, 'rad', axis=0, tiled=True)  39.2 us
    dot_general x1, matrix products, per_cycle(): jnp.einsum('lq,pq->lp', lines_one, table, precision=lax.Precision.HIGHEST)  22.5 us
    all_gather x1, blocking collectives, body(): portion = lax.all_gather(my_cycles, 'sec', axis=2, tiled=True)  16.8 us
    ppermute x3, waiting for transfers between devices, padded_2(): before = lax.ppermute(last, axis, up)  12.4 us
    ppermute x3, starting transfers between devices, padded_2(): before = lax.ppermute(last, axis, up)  10.5 us
    ppermute x3, starting transfers between devices, padded_2(): after = lax.ppermute(first, axis, down)  9.68 us
    ppermute x3, waiting for transfers between devices, padded_2(): after = lax.ppermute(first, axis, down)  7.38 us
  transfers between devices with their start and end apart: 7, of which 6 were waited for; matrix products, arithmetic and copies ran while one was open for 1% of the time, Pallas kernels for 0%

profile of v1, /device:TPU:6, one launch (start us, length us, event | category | flops | bytes accessed | tf_op | source)
XLA Modules:
  0.0 243.8 jit_solution(2670346385443575479)
XLA Ops:
  6.5 1.3 fusion.47
  7.8 3.5 %collective-permute-start = (f32[5,2,64,1]{3,2,1,0:T(8,128)S(1)}, f32[5,2,64,1]{3,2,1,0:T(8,128)S(1)}, u32[]{:S(2)}, u32[]{:S(2)}) collective-permute-start(f32[5,2,64,1]{3,2,1,0:T(8,128)S(1)} %get-tuple-element.59), channel_id=1, source_target_pairs={{0,64},{64,128},{128,192},{192,256},{256,320},{320,384},{384,448},... | collective-permute-start | bytes 7688 | tf_op jit(solution)/shard_map/ppermute | solution.py:25
  11.3 3.8 %collective-permute-start.1 = (f32[5,2,64,1]{3,2,1,0:T(8,128)S(1)}, f32[5,2,64,1]{3,2,1,0:T(8,128)S(1)}, u32[]{:S(2)}, u32[]{:S(2)}) collective-permute-start(f32[5,2,64,1]{3,2,1,0:T(8,128)S(1)} %get-tuple-element.60), channel_id=1, source_target_pairs={{64,0},{128,64},{192,128},{256,192},{320,256},{384,320},{448,384},... | collective-permute-start | bytes 7688 | tf_op jit(solution)/shard_map/ppermute | solution.py:26
  15.3 5.6 %collective-permute-done = f32[5,2,64,1]{3,2,1,0:T(8,128)S(1)} collective-permute-done((f32[5,2,64,1]{3,2,1,0:T(8,128)S(1)}, f32[5,2,64,1]{3,2,1,0:T(8,128)S(1)}, u32[]{:S(2)}, u32[]{:S(2)}) %collective-permute-start) | collective-permute-done | bytes 2592 | tf_op jit(solution)/shard_map/ppermute | solution.py:25
  20.9 1.5 collective-permute-done.1
  22.4 1.1 pad_maximum_fusion.5
  23.5 5.1 %collective-permute-start.2 = (f32[5,2,1,258]{3,2,1,0:T(1,128)S(1)}, f32[5,2,1,258]{3,2,1,0:T(1,128)S(1)}, u32[]{:S(2)}, u32[]{:S(2)}) collective-permute-start(f32[5,2,1,258]{3,2,1,0:T(1,128)S(1)} %get-tuple-element.53), channel_id=1, source_target_pairs={{0,4},{4,8},{8,12},{12,16},{16,20},{20,24},{24,28},{28,32},{32,36}... | collective-permute-start | bytes 30968 | tf_op jit(solution)/shard_map/ppermute | solution.py:25
  28.6 2.2 collective-permute-start.3
  30.9 5.8 %collective-permute-done.3 = f32[5,2,1,258]{3,2,1,0:T(1,128)S(1)} collective-permute-done((f32[5,2,1,258]{3,2,1,0:T(1,128)S(1)}, f32[5,2,1,258]{3,2,1,0:T(1,128)S(1)}, u32[]{:S(2)}, u32[]{:S(2)}) %collective-permute-start.3) | collective-permute-done | bytes 10352 | tf_op jit(solution)/shard_map/ppermute | solution.py:26
  36.6 0.5 pad_maximum_fusion.1
  37.2 0.5 copy.5
  37.7 1.9 collective-permute-start.4
  39.6 0.5 copy.6
  40.2 3.6 %collective-permute-start.5 = (f32[5,1,66,258]{3,1,2,0:T(1,128)S(1)}, f32[5,1,66,258]{3,1,2,0:T(1,128)S(1)}, u32[]{:S(2)}, u32[]{:S(2)}) collective-permute-start(f32[5,1,66,258]{3,1,2,0:T(1,128)S(1)} %copy.6), channel_id=1, source_target_pairs={{1,0},{2,1},{3,2},{0,3},{5,4},{6,5},{7,6},{4,7},{9,8},{10,9},{11,1... | collective-permute-start | bytes 1021688 | tf_op jit(solution)/shard_map/ppermute | solution.py:26
  44.0 6.7 %collective-permute-done.4 = f32[5,1,66,258]{3,1,2,0:T(1,128)S(1)} collective-permute-done((f32[5,1,66,258]{3,1,2,0:T(1,128)S(1)}, f32[5,1,66,258]{3,1,2,0:T(1,128)S(1)}, u32[]{:S(2)}, u32[]{:S(2)}) %collective-permute-start.4) | collective-permute-done | bytes 340592 | tf_op jit(solution)/shard_map/ppermute | solution.py:25
  50.9 0.5 pad_maximum_fusion
  51.4 0.2 slice_bitcast_fusion.3
  51.7 0.2 fusion.28
  51.9 0.3 add_dynamic-update-slice_fusion.2
  52.8 0.4 broadcast_multiply_fusion
  53.3 0.3 fusion.32
  53.6 1.1 fusion.19
  54.7 0.7 slice_select_fusion.1
  55.4 0.6 fusion.44
  58.5 0.7 and_select_fusion
  59.2 0.7 add_select_fusion.1
  59.9 95.5 %all-gather.4.cloned.1.call-done = f32[16,16,10,256]{3,1,2,0:T(8,128)} async-done(((f32[1,16,10,256]{3,1,2,0:T(8,128)}), f32[16,16,10,256]{3,1,2,0:T(8,128)}) %all-gather.4.cloned.1.call-update) | async-done | bytes 2621456 | tf_op jit(solution)/shard_map/all_gather | solution.py:13
  155.5 2.0 reduce_sum.18
  157.5 16.8 %all_gather.11 = f32[1,10,2048]{2,0,1:T(1,128)S(1)} all-gather(f32[1,10,256]{2,0,1:T(1,128)S(1)} %constant_dynamic-slice_fusion), channel_id=1, replica_groups=mesh['sec'=8,'rad'=16,'ax'=4] {'sec'}, dimensions={2}, use_global_device_ids=true | all-gather | bytes 92160 | tf_op jit(solution)/shard_map/all_gather | solution.py:159
  174.2 22.5 %fusion.7 = f32[1,10,256]{2,1,0:T(8,128)S(1)} fusion(f32[]{:T(128)S(6)} %mul.233, f32[]{:T(128)S(6)} %convert_element_type.66, f32[]{:T(128)} %bitcast.13, s32[]{:T(128)S(6)} %select_n.139, s32[2048]{0:T(1024)S(1)} %add_select_fusion.1, s32[256]{0:T(256)S(1)} %and_select_fusion, pred[]{:T(512)S(6)} %lt.63, f32[1,10,2048]{2,0,1:T(1,128)S(1)} %all_gather.11), kind=kOutput, calls=%fused_computation.10 | convolution fusion | flops 70254592 | bytes 101393 | tf_op jit(solution)/shard_map/while/body/eval_jaxpr/lq,pq->lp/dot_general | solution.py:165
  196.8 39.2 %all-gather.1 = f32[16,10,256]{2,1,0:T(8,128)S(1)} all-gather(f32[1,10,256]{2,1,0:T(8,128)S(1)} %fusion.7), channel_id=2, replica_groups=mesh['sec'=8,'rad'=16,'ax'=4] {'rad'}, dimensions={0}, use_global_device_ids=true | all-gather | bytes 174080 | tf_op jit(solution)/shard_map/all_gather | solution.py:168
  236.1 0.9 pad_maximum_fusion.2
  (33 shorter events, 1.4 us)
Async XLA Ops:
  6.5 30.1 %copy-start = (f32[5,2,64,256]{3,2,1,0:T(8,128)S(1)}, f32[5,2,64,256]{3,2,1,0:T(8,128)}, u32[]{:S(2)}) copy-start(f32[5,2,64,256]{3,2,1,0:T(8,128)} %param.2) | copy-start | bytes 1966084
  6.5 148.9 %all-gather.4.cloned.1.call-start = ((), (), s32[]{:S(2)}) async-start(), calls=%async_computation | async-start | bytes 2785280 | tf_op jit(solution)/shard_map/all_gather | solution.py:13
  7.8 13.1 %collective-permute-start = (f32[5,2,64,1]{3,2,1,0:T(8,128)S(1)}, f32[5,2,64,1]{3,2,1,0:T(8,128)S(1)}, u32[]{:S(2)}, u32[]{:S(2)}) collective-permute-start(f32[5,2,64,1]{3,2,1,0:T(8,128)S(1)} %get-tuple-element.59), channel_id=1, source_target_pairs={{0,64},{64,128},{128,192},{192,256},{256,320},{320,384},{384,448},... | collective-permute-start | bytes 7688 | tf_op jit(solution)/shard_map/ppermute | solution.py:25
  11.3 11.1 %collective-permute-start.1 = (f32[5,2,64,1]{3,2,1,0:T(8,128)S(1)}, f32[5,2,64,1]{3,2,1,0:T(8,128)S(1)}, u32[]{:S(2)}, u32[]{:S(2)}) collective-permute-start(f32[5,2,64,1]{3,2,1,0:T(8,128)S(1)} %get-tuple-element.60), channel_id=1, source_target_pairs={{64,0},{128,64},{192,128},{256,192},{320,256},{384,320},{448,384},... | collective-permute-start | bytes 7688 | tf_op jit(solution)/shard_map/ppermute | solution.py:26
  23.5 7.4 %collective-permute-start.2 = (f32[5,2,1,258]{3,2,1,0:T(1,128)S(1)}, f32[5,2,1,258]{3,2,1,0:T(1,128)S(1)}, u32[]{:S(2)}, u32[]{:S(2)}) collective-permute-start(f32[5,2,1,258]{3,2,1,0:T(1,128)S(1)} %get-tuple-element.53), channel_id=1, source_target_pairs={{0,4},{4,8},{8,12},{12,16},{16,20},{20,24},{24,28},{28,32},{32,36}... | collective-permute-start | bytes 30968 | tf_op jit(solution)/shard_map/ppermute | solution.py:25
  28.6 8.0 %collective-permute-start.3 = (f32[5,2,1,258]{3,2,1,0:T(1,128)S(1)}, f32[5,2,1,258]{3,2,1,0:T(1,128)S(1)}, u32[]{:S(2)}, u32[]{:S(2)}) collective-permute-start(f32[5,2,1,258]{3,2,1,0:T(1,128)S(1)} %get-tuple-element.54), channel_id=1, source_target_pairs={{4,0},{8,4},{12,8},{16,12},{20,16},{24,20},{28,24},{32,28},{36,32}... | collective-permute-start | bytes 30968 | tf_op jit(solution)/shard_map/ppermute | solution.py:26
  37.7 13.0 %collective-permute-start.4 = (f32[5,1,66,258]{3,1,2,0:T(1,128)S(1)}, f32[5,1,66,258]{3,1,2,0:T(1,128)S(1)}, u32[]{:S(2)}, u32[]{:S(2)}) collective-permute-start(f32[5,1,66,258]{3,1,2,0:T(1,128)S(1)} %copy.5), channel_id=1, source_target_pairs={{0,1},{1,2},{2,3},{3,0},{4,5},{5,6},{6,7},{7,4},{8,9},{9,10},{10,1... | collective-permute-start | bytes 1021688 | tf_op jit(solution)/shard_map/ppermute | solution.py:25
  40.2 10.7 %collective-permute-start.5 = (f32[5,1,66,258]{3,1,2,0:T(1,128)S(1)}, f32[5,1,66,258]{3,1,2,0:T(1,128)S(1)}, u32[]{:S(2)}, u32[]{:S(2)}) collective-permute-start(f32[5,1,66,258]{3,1,2,0:T(1,128)S(1)} %copy.6), channel_id=1, source_target_pairs={{1,0},{2,1},{3,2},{0,3},{5,4},{6,5},{7,6},{4,7},{9,8},{10,9},{11,1... | collective-permute-start | bytes 1021688 | tf_op jit(solution)/shard_map/ppermute | solution.py:26
  53.6 1.8 copy-start.1
Sparse Core Ops, SparseCore 0:
  55.5 99.8 all-gather.3
